TPU v7x, 512 devices: a whole 4x4x16 slice. The times are simulated.
512 devices in a mesh: row: 32 (over y, x, core), col: 16 (over z).
Axes of the slice: x: 4, y: 4, z: 16, core: 2. Of those that a mesh axis runs over, the one named last changes fastest.
Arguments:
- ainv_block: float32 [4096, 4096], P('row', 'col'), as said below
- factor: float32 [2, 4096, 1024], P(None, 'row', 'col'), may hold values from -0.8 to 0.8
- block_mask: int32 [2, 32], replicated, may hold values 0 or 1
- diag_inverse: float32 [1024, 2, 1024], P('row', None, 'col'), may hold values from -6 to 6
Outputs:
- ainv_panel: float32 [1024, 2, 4096], P('col', None, 'row')
- ainv_diag: float32 [1024, 2, 1024], P('row', None, 'col')
Inputs may be any that keep to these rules, and one draw needn't show every extreme that they name: `ainv_block`: symmetric, diagonal entries between 2 and 3, off-diagonal entries of order one over the square root of 4096.
All inputs are finite; a program needn't handle non-finite values.
Results may differ from a plain program's by a relative error of at most 0.0001.
Values sent between devices are 32-bit elements; how exact they have to be, the bound alone decides.
A program may use at most 64 MiB of HBM per device.

v0:
```python
import jax
import jax.numpy as jnp
from jax import lax
from jax.sharding import PartitionSpec as P

BLOCK = 128


def from_root(block, axis, owner):
    block = jnp.where(lax.axis_index(axis) == owner, block, jnp.zeros_like(block))
    return lax.psum(block, axis)


def local(ainv_block, factor, block_mask, diag_inverse):
    col_count = lax.axis_size("col")
    row_count = lax.axis_size("row")
    ratio = row_count // col_count
    row_index = lax.axis_index("row")
    col_index = lax.axis_index("col")
    rows = factor.shape[1]
    local_blocks = rows // BLOCK
    local_mask = lax.dynamic_slice_in_dim(block_mask, row_index * local_blocks, local_blocks, 1)
    row_mask = jnp.repeat(local_mask, BLOCK, axis=1).astype(jnp.float32)
    masked = factor * row_mask[:, :, None]
    own_rows = lax.all_gather(masked, "col", axis=2, tiled=True)
    pieces = [from_root(own_rows, "row", ratio * col_index + offset) for offset in range(ratio)]
    column_rows = jnp.concatenate(pieces, axis=1)
    piece = column_rows
    summed = lax.psum_scatter(
        jnp.einsum(
            "ij,sjw->wsi",
            ainv_block,
            piece,
            precision=lax.Precision.HIGHEST,
            preferred_element_type=jnp.float32,
        ),
        "col",
        scatter_dimension=0,
        tiled=True,
    )
    ainv_panel = -(summed * row_mask[None, :, :])
    piece = own_rows
    correction = lax.psum_scatter(
        jnp.einsum(
            "siw,vsi->wsv",
            piece,
            ainv_panel,
            precision=lax.Precision.HIGHEST,
            preferred_element_type=jnp.float32,
        ),
        "row",
        scatter_dimension=0,
        tiled=True,
    )
    return (ainv_panel, diag_inverse - correction)


def solution(mesh):
    placed = (P("row", "col"), P(None, "row", "col"), P(), P("row", None, "col"))
    return jax.shard_map(
        local,
        mesh=mesh,
        in_specs=placed,
        out_specs=(P("col", None, "row"), P("row", None, "col")),
        check_vma=False,
    )
```

profile of v0, /device:TPU:1, one launch (start us, length us, event | category | flops | bytes accessed | tf_op | source)
XLA Modules:
  0.0 445.2 jit_solution(8940846543808888751)
XLA Ops:
  7.2 0.0 copy-start
  7.2 0.0 all-gather.2.cloned.1.call-start
  7.2 0.9 convert_reduce_fusion
  8.1 1.5 broadcast_multiply_fusion
  9.6 0.0 all-gather.2.cloned.1.call-update
  9.7 0.0 all-reduce.7.cloned.1.call-start
  9.7 67.8 %all-gather.2.cloned.1.call-done = f32[2,128,1024]{1,2,0:T(8,128)} async-done(((f32[2,128,64]{1,2,0:T(8,128)}), f32[2,128,1024]{1,2,0:T(8,128)}) %all-gather.2.cloned.1.call-update) | async-done | bytes 1048592 | tf_op jit(solution)/shard_map/all_gather | solution.py:25
  77.5 2.7 broadcast_select_fusion.1
  80.2 0.0 all-reduce.7.cloned.1.call-update
  80.3 0.0 reduce-scatter.2.cloned.1.call-start
  80.3 145.2 %all-reduce.7.cloned.1.call-done = (f32[2,128,1024]{1,2,0:T(8,128)}, f32[2,128,1024]{1,2,0:T(8,128)}) async-done(((f32[2,128,1024]{1,2,0:T(8,128)}, f32[2,128,1024]{1,2,0:T(8,128)}), (f32[2,128,1024]{1,2,0:T(8,128)}, f32[2,128,1024]{1,2,0:T(8,128)})) %all-reduce.7.cloned.1.call-update) | async-done | bytes 2097168 | tf_op jit(solution)/shard_map/psum | solution.py:11
  225.5 0.0 copy-done
  225.5 4.3 fusion.4
  229.8 0.0 copy-start.1
  229.8 0.0 reduce-scatter.2.cloned.1.call-update
  229.8 0.0 all-reduce.5.cloned.1.call-start
  229.9 60.2 %reduce-scatter.2.cloned.1.call-done = f32[64,2,128]{2,0,1:T(8,128)} async-done(((f32[1024,2,128]{2,0,1:T(8,128)}), f32[64,2,128]{2,0,1:T(8,128)}) %reduce-scatter.2.cloned.1.call-update) | async-done | bytes 65552 | tf_op jit(solution)/shard_map/reduce_scatter | solution.py:29
  290.1 0.9 multiply_negate_fusion
  291.0 0.0 copy-done.1
  291.0 1.2 convolution_bitcast_fusion
  292.2 0.0 copy-start.2
  292.3 1.3 copy.9
  293.6 0.0 all-reduce.5.cloned.1.call-update
  293.6 1.3 dynamic-slice
  295.5 0.7 copy.10
  296.2 141.0 %all-reduce.5.cloned.1.call-done = f32[1024,2,64]{2,1,0:T(2,128)} async-done(((f32[1024,2,64]{2,1,0:T(2,128)}), f32[1024,2,64]{2,1,0:T(2,128)}) %all-reduce.5.cloned.1.call-update) | async-done | bytes 524304
  437.2 0.0 copy-done.2
  437.2 1.4 dynamic-slice_subtract_fusion
Async XLA Ops:
  7.2 218.3 %copy-start = (f32[128,256]{1,0:T(8,128)S(1)}, f32[128,256]{1,0:T(8,128)}, u32[]{:S(2)}) copy-start(f32[128,256]{1,0:T(8,128)} %param.4) | copy-start | bytes 393220
  7.2 70.4 %all-gather.2.cloned.1.call-start = ((), (), s32[]{:S(2)}) async-start(), calls=%async_computation.1 | async-start | bytes 1114112 | tf_op jit(solution)/shard_map/all_gather | solution.py:25
  9.7 215.8 %all-reduce.7.cloned.1.call-start = ((), (), s32[]{:S(2)}) async-start(), calls=%async_computation.4 | async-start | bytes 4194304 | tf_op jit(solution)/shard_map/psum | solution.py:11
  80.3 209.8 %reduce-scatter.2.cloned.1.call-start = ((), (), s32[]{:S(2)}) async-start(), calls=%async_computation.2 | async-start | bytes 1114112 | tf_op jit(solution)/shard_map/reduce_scatter | solution.py:29
  229.8 61.2 %copy-start.1 = (f32[2,128,1024]{1,2,0:T(8,128)S(1)}, f32[2,128,1024]{1,2,0:T(8,128)}, u32[]{:S(2)}) copy-start(f32[2,128,1024]{1,2,0:T(8,128)} %all-gather.2.cloned.1.call-done) | copy-start | bytes 3145732
  229.8 207.4 %all-reduce.5.cloned.1.call-start = ((), (), s32[]{:S(2)}) async-start(), calls=%async_computation.3 | async-start | bytes 2097152
  292.2 145.0 %copy-start.2 = (f32[32,2,64]{2,1,0:T(2,128)S(1)}, f32[32,2,64]{2,1,0:T(2,128)}, u32[]{:S(2)}) copy-start(f32[32,2,64]{2,1,0:T(2,128)} %param.7) | copy-start | bytes 49156
Sparse Core Ops, SparseCore 0:
  10.7 66.8 all-gather.1
  80.8 144.5 all-reduce.6
  230.0 60.0 reduce-scatter.1
  293.7 143.4 all-reduce.4
where the time goes:
time: 446 us; the launch traced here: 445 us
  waiting for transfers between devices  414 us (93%)
  between operations  14.5 us (3%)
  other arithmetic  7.42 us (2%)
  matrix products  5.58 us (1%)
    psum x1, waiting for transfers between devices, from_root(): return lax.psum(block, axis)  145 us
    unnamed x5, waiting for transfers between devices  141 us
    all_gather x1, waiting for transfers between devices, local(): own_rows = lax.all_gather(masked, 'col', axis=2, tiled=True)  67.8 us
    reduce_scatter x1, waiting for transfers between devices, local(): lax.psum_scatter(jnp.einsum('ij,sjw->wsi', ainv_block, piece, precision=l...  60.2 us
  transfers between devices with their start and end apart: 4, of which 4 were waited for; matrix products, arithmetic and copies ran while one was open for 0% of the time, Pallas kernels for 0%

commit v1 on v0

v1 whole, which is shorter than its diff:
```python
import jax
import jax.numpy as jnp
from jax import lax
from jax.experimental import pallas as pl
from jax.experimental.pallas import tpu as pltpu
from jax.sharding import PartitionSpec as P

MESH = pl.DeviceIdType.MESH
SIDE = 4
CHIPS = SIDE * SIDE
DEPTH = 16
LANES = 128
HANDS = {0: (2, 1), 2: (4, 3), 4: (6, 5), 6: (8, 7)}
ORDER = (2, 1, 4, 3, 6, 5, 8, 7)


def split(x):
    high = x.astype(jnp.bfloat16)
    return high, (x - high.astype(jnp.float32)).astype(jnp.bfloat16)


def signs(d):
    return (d,) if d in (0, 8) else (d, -d)


def slot(d):
    return (d + 7) % DEPTH


def kernel(
    a_ref, f_ref, mask_ref, diag_ref, panel_ref, out_ref,
    g, lhs_hi, lhs_lo, a_hi, a_lo, own, give, take, red, got, fin, pin, p_hi, p_lo,
    part, c_take, c_red, c_got,
    z_send, z_recv, x_send, x_recv, r_send, r_recv, t_send, t_recv, c_sems,
):
    row, col = lax.axis_index("row"), lax.axis_index("col")
    core = lax.rem(row, 2)
    chip = row // 2
    cy, cx = chip // SIDE, lax.rem(chip, SIDE)
    mate = (row + 1 - 2 * core, col)

    def along(d):
        return (row, lax.rem(col + d + DEPTH, DEPTH))

    def in_plane(i):
        return lax.rem(cy + i // SIDE, SIDE) * SIDE + lax.rem(cx + i % SIDE, SIDE)

    barrier = pltpu.get_barrier_semaphore()
    for who in [along(d) for d in (1, -1, 2, -2)] + [mate] + [(in_plane(i) * 2 + core, col) for i in range(1, CHIPS)]:
        pl.semaphore_signal(barrier, inc=1, device_id=who, device_id_type=MESH)

    keep = [mask_ref[s, row].astype(jnp.float32) for s in (0, 1)]
    for s in (0, 1):
        g[slot(0), 64 * s : 64 * s + 64] = f_ref[64 * s : 64 * s + 64] * keep[s]
    for half in (0, 1):
        which = pl.multiple_of(lax.rem(core + half, 2) * LANES, LANES)
        hi, lo = split(a_ref[:, pl.ds(which, LANES)])
        a_hi[:, half * LANES : half * LANES + LANES] = hi
        a_lo[:, half * LANES : half * LANES + LANES] = lo
    p_hi[...] = jnp.zeros_like(p_hi)
    p_lo[...] = jnp.zeros_like(p_lo)
    pl.semaphore_wait(barrier, 4 + 1 + CHIPS - 1)

    def hop(a, b):
        return pltpu.make_async_remote_copy(
            g.at[slot(a)], g.at[slot(b)], z_send.at[slot(b)], z_recv.at[slot(b)],
            device_id=along(b - a), device_id_type=MESH,
        )

    hops = {}

    def hand_on(a):
        step = 1 if a >= 0 else -1
        for b in HANDS.get(abs(a), ()):
            hops[b * step] = hop(a, b * step)
            hops[b * step].start()
            if a == 0:
                hops[-b] = hop(0, -b)
                hops[-b].start()

    def arrive(t):
        for d in signs(t):
            hops[d].wait_recv()
            if not (d == -6):
                hand_on(d)
            else:
                hops[-7] = hop(-6, -7)
                hops[-7].start()

    def swap(t):
        n = len(signs(t))
        return pltpu.make_async_remote_copy(
            give.at[t, pl.ds(0, n)], take.at[t, pl.ds(0, n)], x_send.at[t], x_recv.at[t],
            device_id=mate, device_id_type=MESH,
        )

    def multiply(t):
        for n, d in enumerate(signs(t)):
            hi, lo = split(g[slot(d)])
            for s in (0, 1):
                lhs_hi[slot(d), :, s * LANES : s * LANES + LANES] = hi[64 * s : 64 * s + 64]
                lhs_lo[slot(d), :, s * LANES : s * LANES + LANES] = lo[64 * s : 64 * s + 64]
            ah, al = a_hi[...], a_lo[...]
            x = jnp.dot(hi, ah, preferred_element_type=jnp.float32)
            x += jnp.dot(hi, al, preferred_element_type=jnp.float32)
            x += jnp.dot(lo, ah, preferred_element_type=jnp.float32)
            own[t, n] = x[:, :LANES]
            give[t, n] = x[:, LANES:]
        swap(t).start()

    def piece(t, i):
        n = len(signs(t))
        to = in_plane(i)
        return pltpu.make_async_remote_copy(
            red.at[t, to, pl.ds(0, n)], got.at[t, i, pl.ds(0, n)], r_send.at[t], r_recv.at[t],
            device_id=(to * 2 + core, col), device_id_type=MESH,
        )

    def scatter(t):
        swap(t).wait_recv()
        for n, _ in enumerate(signs(t)):
            red[t, :, n] = (own[t, n] + take[t, n]).reshape(CHIPS, 8, LANES)
        for i in range(1, CHIPS):
            piece(t, i).start()

    def home(t, n, d):
        return pltpu.make_async_remote_copy(
            fin.at[t, n], pin.at[chip], t_send, t_recv,
            device_id=(col * 2 + core, lax.rem(col - d + DEPTH, DEPTH)), device_id_type=MESH,
        )

    def finish(t):
        n = len(signs(t))
        arrived = got.at[t, pl.ds(1, CHIPS - 1), pl.ds(0, n)]
        pltpu.make_async_copy(arrived, arrived, r_recv.at[t]).wait()
        for n, d in enumerate(signs(t)):
            total = red[t, chip, n]
            for i in range(1, CHIPS):
                total += got[t, i, n]
            fin[t, n] = total
            if d != 0:
                home(t, n, d).start()
            else:
                @pl.when(chip != col)
                def _():
                    home(0, 0, 0).start()

                @pl.when(chip == col)
                def _():
                    pltpu.make_async_copy(fin.at[0, 0], pin.at[chip], t_recv).start()

    hand_on(0)
    stages = [(0, multiply), (2, arrive), (2, multiply), (0, scatter), (1, arrive), (1, multiply), (2, scatter)]
    stages += [(4, arrive), (4, multiply), (1, scatter), (0, finish), (3, arrive), (3, multiply), (4, scatter), (2, finish)]
    stages += [(6, arrive), (6, multiply), (3, scatter), (1, finish), (5, arrive), (5, multiply), (6, scatter), (4, finish)]
    stages += [(8, arrive), (8, multiply), (5, scatter), (3, finish), (7, arrive), (7, multiply), (8, scatter), (7, scatter)]
    stages += [(6, finish), (5, finish), (8, finish), (7, finish)]
    for t, what in stages:
        what(t)

    pltpu.make_async_copy(pin, pin, t_recv).wait()
    for s in (0, 1):
        block = pin[8 * s : 8 * s + 8].reshape(64, LANES) * keep[s]
        panel_ref[pl.ds(s, 64, stride=2), :] = -block
        hi, lo = split(block)
        p_hi[64 * s : 64 * s + 64, s * LANES : s * LANES + LANES] = hi
        p_lo[64 * s : 64 * s + 64, s * LANES : s * LANES + LANES] = lo

    contract = (((1,), (1,)), ((), ()))
    for n in range(4):
        span = slice(4 * n, 4 * n + 4)
        hi = lhs_hi[span].reshape(256, 2 * LANES)
        lo = lhs_lo[span].reshape(256, 2 * LANES)
        y = lax.dot_general(hi, p_hi[...], contract, preferred_element_type=jnp.float32)
        y += lax.dot_general(hi, p_lo[...], contract, preferred_element_type=jnp.float32)
        y += lax.dot_general(lo, p_hi[...], contract, preferred_element_type=jnp.float32)
        part[span] = y.reshape(4, 2, 32, LANES)

    c_swap = pltpu.make_async_remote_copy(
        part.at[:, 1 - core], c_take, c_sems.at[0], c_sems.at[1], device_id=mate, device_id_type=MESH
    )
    c_swap.start()
    c_swap.wait_recv()
    c_red[...] = part[:, core] + c_take[...]

    def c_piece(i):
        to = in_plane(i)
        return pltpu.make_async_remote_copy(
            c_red.at[lax.rem(col - to + 7 + 2 * DEPTH, DEPTH)], c_got.at[i], c_sems.at[2], c_sems.at[3],
            device_id=(to * 2 + core, col), device_id_type=MESH,
        )

    for i in range(1, CHIPS):
        c_piece(i).start()
    arrived = c_got.at[pl.ds(1, CHIPS - 1)]
    pltpu.make_async_copy(arrived, arrived, c_sems.at[3]).wait()
    total = c_red[lax.rem(col - chip + 7 + 2 * DEPTH, DEPTH)]
    for i in range(1, CHIPS):
        total += c_got[i]
    for s in (0, 1):
        rows = pl.ds(s, 32, stride=2)
        out_ref[rows, :] = diag_ref[rows, :] + total[:, 64 * s : 64 * s + 64]

    for d in hops:
        hops[d].wait_send()
    for t in range(9):
        swap(t).wait_send()
        n = len(signs(t))
        left = got.at[t, pl.ds(1, CHIPS - 1), pl.ds(0, n)]
        pltpu.make_async_copy(left, left, r_send.at[t]).wait()

    @pl.when(chip != col)
    def _():
        pltpu.make_async_copy(pin, pin, t_send).wait()

    @pl.when(chip == col)
    def _():
        left = pin.at[pl.ds(0, CHIPS - 1)]
        pltpu.make_async_copy(left, left, t_send).wait()

    c_swap.wait_send()
    pltpu.make_async_copy(arrived, arrived, c_sems.at[2]).wait()


def local(ainv_block, factor, block_mask, diag_inverse):
    f = jnp.transpose(factor, (0, 2, 1)).reshape(128, 128)
    diag = diag_inverse.reshape(64, 64)
    f32, bf16 = jnp.float32, jnp.bfloat16
    vmem = pl.BlockSpec(memory_space=pltpu.VMEM)
    dma = pltpu.SemaphoreType.DMA
    panel, out = pl.pallas_call(
        kernel,
        out_shape=(jax.ShapeDtypeStruct((128, 128), f32), jax.ShapeDtypeStruct((64, 64), f32)),
        in_specs=[vmem, vmem, pl.BlockSpec(memory_space=pltpu.SMEM), vmem],
        out_specs=(vmem, vmem),
        scratch_shapes=[
            pltpu.VMEM((DEPTH, 128, LANES), f32),
            pltpu.VMEM((DEPTH, 64, 256), bf16),
            pltpu.VMEM((DEPTH, 64, 256), bf16),
            pltpu.VMEM((128, 256), bf16),
            pltpu.VMEM((128, 256), bf16),
            pltpu.VMEM((9, 2, 128, LANES), f32),
            pltpu.VMEM((9, 2, 128, LANES), f32),
            pltpu.VMEM((9, 2, 128, LANES), f32),
            pltpu.VMEM((9, CHIPS, 2, 8, LANES), f32),
            pltpu.VMEM((9, CHIPS, 2, 8, LANES), f32),
            pltpu.VMEM((9, 2, 8, LANES), f32),
            pltpu.VMEM((CHIPS, 8, LANES), f32),
            pltpu.VMEM((128, 256), bf16),
            pltpu.VMEM((128, 256), bf16),
            pltpu.VMEM((DEPTH, 2, 32, LANES), f32),
            pltpu.VMEM((DEPTH, 32, LANES), f32),
            pltpu.VMEM((DEPTH, 32, LANES), f32),
            pltpu.VMEM((CHIPS, 32, LANES), f32),
            dma((DEPTH,)), dma((DEPTH,)), dma((9,)), dma((9,)), dma((9,)), dma((9,)), dma, dma, dma((4,)),
        ],
        compiler_params=pltpu.CompilerParams(collective_id=0, has_side_effects=True, vmem_limit_bytes=40 * 2**20),
        cost_estimate=pl.CostEstimate(flops=3 * 2 * 84 * 2**20, bytes_accessed=2**20, transcendentals=0),
    )(ainv_block, f, block_mask, diag)
    return panel.reshape(64, 2, 128), out.reshape(32, 2, 64)


def solution(mesh):
    placed = (P("row", "col"), P(None, "row", "col"), P(), P("row", None, "col"))
    return jax.shard_map(
        local,
        mesh=mesh,
        in_specs=placed,
        out_specs=(P("col", None, "row"), P("row", None, "col")),
        check_vma=False,
    )
```

time: 446 us -> 64.3 us (0.14)
  waiting for transfers between devices: 414 us -> 0 us
  Pallas kernels: 0 us -> 59 us
  between operations: 14.5 us -> 0.65 us
  other arithmetic: 7.42 us -> 0 us
  matrix products: 5.58 us -> 0 us
    psum x1 -> x0, waiting for transfers between devices: 145 us -> none  [from_root(): return lax.psum(block, axis)]
    unnamed x5 -> x0, waiting for transfers between devices: 141 us -> none
    all_gather x1 -> x0, waiting for transfers between devices: 67.8 us -> none  [local(): own_rows = lax.all_gather(masked, 'col', axis=2, tiled=True)]
    reduce_scatter x1 -> x0, waiting for transfers between devices: 60.2 us -> none  [local(): lax.psum_scatter(jnp.einsum('ij,sjw->wsi', ainv_block, piece, precision=l...]
    pallas_call x0 -> x1, Pallas kernels: none -> 59 us  [local(): pl.pallas_call(kernel, out_shape=(jax.ShapeDtypeStruct((128, 128), f32),...]
    dot_general x2 -> x0, matrix products: 5.58 us -> none  [the longest x1 4.33 us: local(): jnp.einsum('ij,sjw->wsi', ainv_block, piece, precision=lax.Precision.HIGH...]
  transfers between devices with their start and end apart: 4 -> 0, of which waited for: 4 -> 0; matrix products, arithmetic and copies ran while one was open for 0% -> 0% of each run, Pallas kernels for 0% -> 0%
where the time goes in v1:
time: 64.3 us; the launch traced here: 64.1 us
  Pallas kernels  59 us (92%)
  local copies, waits for them, and re-layouts  4.42 us (7%)
  between operations  0.65 us (1%)
    pallas_call x1, Pallas kernels, local(): pl.pallas_call(kernel, out_shape=(jax.ShapeDtypeStruct((128, 128), f32),...  59 us
    unnamed x10, local copies, waits for them, and re-layouts  4.42 us

profile of v1, /device:TPU:1, one launch (start us, length us, event | category | flops | bytes accessed | tf_op | source)
XLA Modules:
  0.0 64.1 jit_solution(7328551954080378769)
XLA Ops:
  0.6 0.0 copy-start.3
  0.6 0.7 %copy-done.3 = s32[2,32]{1,0:T(2,128)S(1)} copy-done((s32[2,32]{1,0:T(2,128)S(1)}, s32[2,32]{1,0:T(2,128)}, u32[]{:S(2)}) %copy-start.3) | copy-done | bytes 280
  1.3 0.0 copy-start
  1.3 0.9 %copy-done = f32[128,256]{1,0:T(8,128)S(1)} copy-done((f32[128,256]{1,0:T(8,128)S(1)}, f32[128,256]{1,0:T(8,128)}, u32[]{:S(2)}) %copy-start) | copy-done | bytes 131096
  2.2 0.0 copy-start.1
  2.2 0.8 %copy-done.1 = f32[2,128,64]{1,2,0:T(8,128)S(1)} copy-done((f32[2,128,64]{1,2,0:T(8,128)S(1)}, f32[2,128,64]{1,2,0:T(8,128)}, u32[]{:S(2)}) %copy-start.1) | copy-done | bytes 65560
  3.1 0.0 copy-start.2
  3.1 0.8 %copy-done.2 = f32[32,2,64]{2,1,0:T(2,128)S(1)} copy-done((f32[32,2,64]{2,1,0:T(2,128)S(1)}, f32[32,2,64]{2,1,0:T(2,128)}, u32[]{:S(2)}) %copy-start.2) | copy-done | bytes 16408
  3.8 59.0 %shard_map.59 = (f32[128,128]{1,0:T(8,128)S(1)}, f32[64,64]{1,0:T(8,128)S(1)}) custom-call(f32[128,256]{1,0:T(8,128)S(1)} %copy-done, f32[128,128]{1,0:T(8,128)S(1)} %bitcast.8, s32[2,32]{1,0:T(2,128)S(1)} %copy-done.3, f32[64,64]{1,0:T(8,128)S(1)} %bitcast.9), custom_call_target="tpu_custom_call" | custom-call | flops 528482304 | bytes 1048576 | tf_op jit(solution)/shard_map/pallas_call | solution.py:231
  62.8 0.6 copy.8
  63.4 0.6 copy.9
Async XLA Ops:
  0.6 0.7 %copy-start.3 = (s32[2,32]{1,0:T(2,128)S(1)}, s32[2,32]{1,0:T(2,128)}, u32[]{:S(2)}) copy-start(s32[2,32]{1,0:T(2,128)} %mask_ref.1) | copy-start | bytes 772
  1.3 0.9 %copy-start = (f32[128,256]{1,0:T(8,128)S(1)}, f32[128,256]{1,0:T(8,128)}, u32[]{:S(2)}) copy-start(f32[128,256]{1,0:T(8,128)} %a_ref.1) | copy-start | bytes 393220
  2.2 0.8 %copy-start.1 = (f32[2,128,64]{1,2,0:T(8,128)S(1)}, f32[2,128,64]{1,2,0:T(8,128)}, u32[]{:S(2)}) copy-start(f32[2,128,64]{1,2,0:T(8,128)} %param.5) | copy-start | bytes 196612
  3.1 0.8 %copy-start.2 = (f32[32,2,64]{2,1,0:T(2,128)S(1)}, f32[32,2,64]{2,1,0:T(2,128)}, u32[]{:S(2)}) copy-start(f32[32,2,64]{2,1,0:T(2,128)} %param.7) | copy-start | bytes 49156

commit v2 on v1

--- a/solution.py
+++ b/solution.py
@@ -10,8 +10,16 @@
 CHIPS = SIDE * SIDE
 DEPTH = 16
 LANES = 128
+PARTS = 4
 HANDS = {0: (2, 1), 2: (4, 3), 4: (6, 5), 6: (8, 7)}
 ORDER = (2, 1, 4, 3, 6, 5, 8, 7)
+
+
+def far(i):
+    return min(i // SIDE, SIDE - i // SIDE) + min(i % SIDE, SIDE - i % SIDE)
+
+
+OTHERS = sorted(range(1, CHIPS), key=far, reverse=True)
 
 
 def split(x):
@@ -28,10 +36,11 @@
 
 
 def kernel(
-    a_ref, f_ref, mask_ref, diag_ref, panel_ref, out_ref,
+    a_hbm, f_hbm, mask_hbm, diag_hbm, panel_ref, out_ref,
+    a_ref, f_ref, mask_ref, diag_ref,
     g, lhs_hi, lhs_lo, a_hi, a_lo, own, give, take, red, got, fin, pin, p_hi, p_lo,
     part, c_take, c_red, c_got,
-    z_send, z_recv, x_send, x_recv, r_send, r_recv, t_send, t_recv, c_sems,
+    in_sems, z_send, z_recv, x_send, x_recv, r_send, r_recv, t_send, t_recv, cx_send, cx_recv, c_sems,
 ):
     row, col = lax.axis_index("row"), lax.axis_index("col")
     core = lax.rem(row, 2)
@@ -45,10 +54,20 @@
     def in_plane(i):
         return lax.rem(cy + i // SIDE, SIDE) * SIDE + lax.rem(cx + i % SIDE, SIDE)
 
+    loads = [
+        pltpu.make_async_copy(mask_hbm, mask_ref, in_sems.at[0]),
+        pltpu.make_async_copy(f_hbm, f_ref, in_sems.at[1]),
+        pltpu.make_async_copy(a_hbm, a_ref, in_sems.at[2]),
+        pltpu.make_async_copy(diag_hbm, diag_ref, in_sems.at[3]),
+    ]
+    for load in loads:
+        load.start()
     barrier = pltpu.get_barrier_semaphore()
     for who in [along(d) for d in (1, -1, 2, -2)] + [mate] + [(in_plane(i) * 2 + core, col) for i in range(1, CHIPS)]:
         pl.semaphore_signal(barrier, inc=1, device_id=who, device_id_type=MESH)
 
+    for load in loads:
+        load.wait()
     keep = [mask_ref[s, row].astype(jnp.float32) for s in (0, 1)]
     for s in (0, 1):
         g[slot(0), 64 * s : 64 * s + 64] = f_ref[64 * s : 64 * s + 64] * keep[s]
@@ -62,9 +81,12 @@
     pl.semaphore_wait(barrier, 4 + 1 + CHIPS - 1)
 
     def hop(a, b):
-        return pltpu.make_async_remote_copy(
-            g.at[slot(a)], g.at[slot(b)], z_send.at[slot(b)], z_recv.at[slot(b)],
-            device_id=along(b - a), device_id_type=MESH,
+        source, dest = g.at[slot(a)], g.at[slot(b)]
+        if abs(b) == 8:
+            half = pl.ds(0 if b > 0 else 64, 64)
+            source, dest = g.at[slot(a), half], g.at[slot(b), half]
+        return pltpu.make_async_remote_copy(
+            source, dest, z_send.at[b + 8], z_recv.at[b + 8], device_id=along(b - a), device_id_type=MESH
         )
 
     hops = {}
@@ -79,13 +101,9 @@
                 hops[-b].start()
 
     def arrive(t):
-        for d in signs(t):
+        for d in (t, -t):
             hops[d].wait_recv()
-            if not (d == -6):
-                hand_on(d)
-            else:
-                hops[-7] = hop(-6, -7)
-                hops[-7].start()
+            hand_on(d)
 
     def swap(t):
         n = len(signs(t))
@@ -120,7 +138,7 @@
         swap(t).wait_recv()
         for n, _ in enumerate(signs(t)):
             red[t, :, n] = (own[t, n] + take[t, n]).reshape(CHIPS, 8, LANES)
-        for i in range(1, CHIPS):
+        for i in OTHERS:
             piece(t, i).start()
 
     def home(t, n, d):
@@ -150,11 +168,7 @@
                     pltpu.make_async_copy(fin.at[0, 0], pin.at[chip], t_recv).start()
 
     hand_on(0)
-    stages = [(0, multiply), (2, arrive), (2, multiply), (0, scatter), (1, arrive), (1, multiply), (2, scatter)]
-    stages += [(4, arrive), (4, multiply), (1, scatter), (0, finish), (3, arrive), (3, multiply), (4, scatter), (2, finish)]
-    stages += [(6, arrive), (6, multiply), (3, scatter), (1, finish), (5, arrive), (5, multiply), (6, scatter), (4, finish)]
-    stages += [(8, arrive), (8, multiply), (5, scatter), (3, finish), (7, arrive), (7, multiply), (8, scatter), (7, scatter)]
-    stages += [(6, finish), (5, finish), (8, finish), (7, finish)]
+    stages = [(0, multiply), (2, arrive), (2, multiply), (1, arrive), (1, multiply), (4, arrive), (0, scatter), (2, scatter), (1, scatter), (4, multiply), (3, arrive), (3, multiply), (6, arrive), (4, scatter), (3, scatter), (6, multiply), (5, arrive), (5, multiply), (0, finish), (2, finish), (1, finish), (6, scatter), (5, scatter), (8, arrive), (8, multiply), (7, arrive), (7, multiply), (8, scatter), (7, scatter), (4, finish), (3, finish), (6, finish), (5, finish), (8, finish), (7, finish)]
     for t, what in stages:
         what(t)
 
@@ -167,36 +181,45 @@
         p_lo[64 * s : 64 * s + 64, s * LANES : s * LANES + LANES] = lo
 
     contract = (((1,), (1,)), ((), ()))
-    for n in range(4):
-        span = slice(4 * n, 4 * n + 4)
-        hi = lhs_hi[span].reshape(256, 2 * LANES)
-        lo = lhs_lo[span].reshape(256, 2 * LANES)
+    many = DEPTH // PARTS
+
+    def c_swap(n):
+        span = pl.ds(many * n, many)
+        return pltpu.make_async_remote_copy(
+            part.at[span, 1 - core], c_take.at[span], cx_send.at[n], cx_recv.at[n], device_id=mate, device_id_type=MESH
+        )
+
+    def target(k):
+        return lax.rem(col - k + 7 + 2 * DEPTH, DEPTH)
+
+    def c_piece(k):
+        return pltpu.make_async_remote_copy(
+            c_red.at[k], c_got.at[chip], c_sems.at[0], c_sems.at[1],
+            device_id=(target(k) * 2 + core, col), device_id_type=MESH,
+        )
+
+    for n in range(PARTS):
+        span = slice(many * n, many * n + many)
+        hi = lhs_hi[span].reshape(64 * many, 2 * LANES)
+        lo = lhs_lo[span].reshape(64 * many, 2 * LANES)
         y = lax.dot_general(hi, p_hi[...], contract, preferred_element_type=jnp.float32)
         y += lax.dot_general(hi, p_lo[...], contract, preferred_element_type=jnp.float32)
         y += lax.dot_general(lo, p_hi[...], contract, preferred_element_type=jnp.float32)
-        part[span] = y.reshape(4, 2, 32, LANES)
-
-    c_swap = pltpu.make_async_remote_copy(
-        part.at[:, 1 - core], c_take, c_sems.at[0], c_sems.at[1], device_id=mate, device_id_type=MESH
-    )
-    c_swap.start()
-    c_swap.wait_recv()
-    c_red[...] = part[:, core] + c_take[...]
-
-    def c_piece(i):
-        to = in_plane(i)
-        return pltpu.make_async_remote_copy(
-            c_red.at[lax.rem(col - to + 7 + 2 * DEPTH, DEPTH)], c_got.at[i], c_sems.at[2], c_sems.at[3],
-            device_id=(to * 2 + core, col), device_id_type=MESH,
-        )
-
-    for i in range(1, CHIPS):
-        c_piece(i).start()
-    arrived = c_got.at[pl.ds(1, CHIPS - 1)]
-    pltpu.make_async_copy(arrived, arrived, c_sems.at[3]).wait()
+        part[span] = y.reshape(many, 2, 32, LANES)
+        c_swap(n).start()
+    for n in range(PARTS):
+        span = slice(many * n, many * n + many)
+        c_swap(n).wait_recv()
+        c_red[span] = part[span, core] + c_take[span]
+        for k in range(many * n, many * n + many):
+            @pl.when(target(k) != chip)
+            def _():
+                c_piece(k).start()
+    most = c_got.at[pl.ds(0, CHIPS - 1)]
+    pltpu.make_async_copy(most, most, c_sems.at[1]).wait()
     total = c_red[lax.rem(col - chip + 7 + 2 * DEPTH, DEPTH)]
-    for i in range(1, CHIPS):
-        total += c_got[i]
+    for i in range(CHIPS):
+        total += jnp.where(chip == i, jnp.zeros_like(total), c_got[i])
     for s in (0, 1):
         rows = pl.ds(s, 32, stride=2)
         out_ref[rows, :] = diag_ref[rows, :] + total[:, 64 * s : 64 * s + 64]
@@ -218,8 +241,17 @@
         left = pin.at[pl.ds(0, CHIPS - 1)]
         pltpu.make_async_copy(left, left, t_send).wait()
 
-    c_swap.wait_send()
-    pltpu.make_async_copy(arrived, arrived, c_sems.at[2]).wait()
+    for n in range(PARTS):
+        c_swap(n).wait_send()
+    pltpu.make_async_copy(most, most, c_sems.at[0]).wait()
+
+
+def hand_out(panel_in, out_in, panel, out, sems):
+    copies = [pltpu.make_async_copy(panel_in, panel, sems.at[0]), pltpu.make_async_copy(out_in, out, sems.at[1])]
+    for copy in copies:
+        copy.start()
+    for copy in copies:
+        copy.wait()
 
 
 def local(ainv_block, factor, block_mask, diag_inverse):
@@ -231,9 +263,13 @@
     panel, out = pl.pallas_call(
         kernel,
         out_shape=(jax.ShapeDtypeStruct((128, 128), f32), jax.ShapeDtypeStruct((64, 64), f32)),
-        in_specs=[vmem, vmem, pl.BlockSpec(memory_space=pltpu.SMEM), vmem],
+        in_specs=[pl.BlockSpec(memory_space=pltpu.HBM)] * 4,
         out_specs=(vmem, vmem),
         scratch_shapes=[
+            pltpu.VMEM((128, 256), f32),
+            pltpu.VMEM((128, LANES), f32),
+            pltpu.SMEM((2, 32), jnp.int32),
+            pltpu.VMEM((64, 64), f32),
             pltpu.VMEM((DEPTH, 128, LANES), f32),
             pltpu.VMEM((DEPTH, 64, 256), bf16),
             pltpu.VMEM((DEPTH, 64, 256), bf16),
@@ -252,11 +288,19 @@
             pltpu.VMEM((DEPTH, 32, LANES), f32),
             pltpu.VMEM((DEPTH, 32, LANES), f32),
             pltpu.VMEM((CHIPS, 32, LANES), f32),
-            dma((DEPTH,)), dma((DEPTH,)), dma((9,)), dma((9,)), dma((9,)), dma((9,)), dma, dma, dma((4,)),
+            dma((4,)), dma((DEPTH + 1,)), dma((DEPTH + 1,)), dma((9,)), dma((9,)), dma((9,)), dma((9,)), dma, dma, dma((PARTS,)), dma((PARTS,)), dma((2,)),
         ],
-        compiler_params=pltpu.CompilerParams(collective_id=0, has_side_effects=True, vmem_limit_bytes=40 * 2**20),
+        compiler_params=pltpu.CompilerParams(collective_id=0, has_side_effects=True, vmem_limit_bytes=63 * 2**20),
         cost_estimate=pl.CostEstimate(flops=3 * 2 * 84 * 2**20, bytes_accessed=2**20, transcendentals=0),
     )(ainv_block, f, block_mask, diag)
+    hbm = pl.BlockSpec(memory_space=pltpu.HBM)
+    panel, out = pl.pallas_call(
+        hand_out,
+        out_shape=(jax.ShapeDtypeStruct((128, 128), f32), jax.ShapeDtypeStruct((64, 64), f32)),
+        in_specs=[vmem, vmem],
+        out_specs=(hbm, hbm),
+        scratch_shapes=[dma((2,))],
+    )(panel, out)
     return panel.reshape(64, 2, 128), out.reshape(32, 2, 64)
 
 

time: 64.3 us -> 60.1 us (0.935)
  local copies, waits for them, and re-layouts: 4.42 us -> 0 us
    unnamed x10 -> x0, local copies, waits for them, and re-layouts: 4.42 us -> none
    pallas_call x1, Pallas kernels: 59 us -> 57.3 us  [local(): pl.pallas_call(kernel, out_shape=(jax.ShapeDtypeStruct((128, 128), f32),...]
    pallas_call x0 -> x1, Pallas kernels: none -> 1.49 us  [local(): pl.pallas_call(hand_out, out_shape=(jax.ShapeDtypeStruct((128, 128), f32)...]
where the time goes in v2:
time: 60.1 us; the launch traced here: 59.4 us
  Pallas kernels  58.8 us (98%)
  between operations  0.64 us (1%)
    pallas_call x1, Pallas kernels, local(): pl.pallas_call(kernel, out_shape=(jax.ShapeDtypeStruct((128, 128), f32),...  57.3 us
    pallas_call x1, Pallas kernels, local(): pl.pallas_call(hand_out, out_shape=(jax.ShapeDtypeStruct((128, 128), f32)...  1.49 us

profile of v2, /device:TPU:1, one launch (start us, length us, event | category | flops | bytes accessed | tf_op | source)
XLA Modules:
  0.0 59.4 jit_solution(12254301816606776675)
XLA Ops:
  0.6 57.3 %shard_map.59 = (f32[128,128]{1,0:T(8,128)}, f32[64,64]{1,0:T(8,128)}) custom-call(f32[128,256]{1,0:T(8,128)} %a_hbm.1, f32[128,128]{1,0:T(8,128)} %bitcast.6, s32[2,32]{1,0:T(2,128)} %mask_hbm.1, f32[64,64]{1,0:T(8,128)} %bitcast.8), custom_call_target="tpu_custom_call" | custom-call | flops 528482304 | bytes 1048576 | tf_op jit(solution)/shard_map/pallas_call | solution.py:263
  57.9 1.5 %shard_map.60 = (f32[128,128]{1,0:T(8,128)}, f32[64,64]{1,0:T(8,128)}) custom-call(f32[128,128]{1,0:T(8,128)} %get-tuple-element.6.panel_in, f32[64,64]{1,0:T(8,128)} %get-tuple-element.7.out_in), custom_call_target="tpu_custom_call" | custom-call | tf_op jit(solution)/shard_map/pallas_call | solution.py:297

commit v3 on v2

--- a/solution.py
+++ b/solution.py
@@ -10,7 +10,7 @@
 CHIPS = SIDE * SIDE
 DEPTH = 16
 LANES = 128
-PARTS = 4
+PARTS = 8
 HANDS = {0: (2, 1), 2: (4, 3), 4: (6, 5), 6: (8, 7)}
 ORDER = (2, 1, 4, 3, 6, 5, 8, 7)
 
@@ -40,7 +40,7 @@
     a_ref, f_ref, mask_ref, diag_ref,
     g, lhs_hi, lhs_lo, a_hi, a_lo, own, give, take, red, got, fin, pin, p_hi, p_lo,
     part, c_take, c_red, c_got,
-    in_sems, z_send, z_recv, x_send, x_recv, r_send, r_recv, t_send, t_recv, cx_send, cx_recv, c_sems,
+    in_sems, z_send, z_recv, x_send, x_recv, r_send, r_recv, t_send, t_recv, cx_send, cx_recv, c_sems, ready,
 ):
     row, col = lax.axis_index("row"), lax.axis_index("col")
     core = lax.rem(row, 2)
@@ -63,7 +63,7 @@
     for load in loads:
         load.start()
     barrier = pltpu.get_barrier_semaphore()
-    for who in [along(d) for d in (1, -1, 2, -2)] + [mate] + [(in_plane(i) * 2 + core, col) for i in range(1, CHIPS)]:
+    for who in [along(d) for d in (1, -1, 2, -2)] + [mate] + [(in_plane(i) * 2 + core, col) for i in (1, 2, 3, 4, 8, 12)]:
         pl.semaphore_signal(barrier, inc=1, device_id=who, device_id_type=MESH)
 
     for load in loads:
@@ -78,7 +78,7 @@
         a_lo[:, half * LANES : half * LANES + LANES] = lo
     p_hi[...] = jnp.zeros_like(p_hi)
     p_lo[...] = jnp.zeros_like(p_lo)
-    pl.semaphore_wait(barrier, 4 + 1 + CHIPS - 1)
+    pl.semaphore_wait(barrier, 4 + 1 + 6)
 
     def hop(a, b):
         source, dest = g.at[slot(a)], g.at[slot(b)]
@@ -135,6 +135,8 @@
         )
 
     def scatter(t):
+        if t == 0:
+            pl.semaphore_wait(ready, SIDE - 1)
         swap(t).wait_recv()
         for n, _ in enumerate(signs(t)):
             red[t, :, n] = (own[t, n] + take[t, n]).reshape(CHIPS, 8, LANES)
@@ -168,7 +170,9 @@
                     pltpu.make_async_copy(fin.at[0, 0], pin.at[chip], t_recv).start()
 
     hand_on(0)
-    stages = [(0, multiply), (2, arrive), (2, multiply), (1, arrive), (1, multiply), (4, arrive), (0, scatter), (2, scatter), (1, scatter), (4, multiply), (3, arrive), (3, multiply), (6, arrive), (4, scatter), (3, scatter), (6, multiply), (5, arrive), (5, multiply), (0, finish), (2, finish), (1, finish), (6, scatter), (5, scatter), (8, arrive), (8, multiply), (7, arrive), (7, multiply), (8, scatter), (7, scatter), (4, finish), (3, finish), (6, finish), (5, finish), (8, finish), (7, finish)]
+    for i in (4, 8, 12):
+        pl.semaphore_signal(ready, inc=1, device_id=(in_plane(i) * 2 + core, col), device_id_type=MESH)
+    stages = [(0, multiply), (2, arrive), (2, multiply), (1, arrive), (0, scatter), (1, multiply), (2, scatter), (4, arrive), (4, multiply), (1, scatter), (3, arrive), (3, multiply), (4, scatter), (0, finish), (6, arrive), (6, multiply), (3, scatter), (2, finish), (5, arrive), (5, multiply), (6, scatter), (1, finish), (5, scatter), (4, finish), (8, arrive), (8, multiply), (7, arrive), (7, multiply), (8, scatter), (7, scatter), (3, finish), (6, finish), (5, finish), (8, finish), (7, finish)]
     for t, what in stages:
         what(t)
 
@@ -181,7 +185,8 @@
         p_lo[64 * s : 64 * s + 64, s * LANES : s * LANES + LANES] = lo
 
     contract = (((1,), (1,)), ((), ()))
-    many = DEPTH // PARTS
+    many = CHIPS // PARTS
+    order = OTHERS + [0]
 
     def c_swap(n):
         span = pl.ds(many * n, many)
@@ -189,19 +194,21 @@
             part.at[span, 1 - core], c_take.at[span], cx_send.at[n], cx_recv.at[n], device_id=mate, device_id_type=MESH
         )
 
-    def target(k):
-        return lax.rem(col - k + 7 + 2 * DEPTH, DEPTH)
+    def block(half, i):
+        to = in_plane(i) if i else chip
+        return half[lax.rem(col - to + 7 + 2 * DEPTH, DEPTH)]
 
     def c_piece(k):
-        return pltpu.make_async_remote_copy(
-            c_red.at[k], c_got.at[chip], c_sems.at[0], c_sems.at[1],
-            device_id=(target(k) * 2 + core, col), device_id_type=MESH,
+        i = order[k]
+        return pltpu.make_async_remote_copy(
+            c_red.at[k], c_got.at[k], c_sems.at[0], c_sems.at[1],
+            device_id=(in_plane(i) * 2 + core, col), device_id_type=MESH,
         )
 
     for n in range(PARTS):
         span = slice(many * n, many * n + many)
-        hi = lhs_hi[span].reshape(64 * many, 2 * LANES)
-        lo = lhs_lo[span].reshape(64 * many, 2 * LANES)
+        hi = jnp.concatenate([block(lhs_hi, i) for i in order[span]], axis=0)
+        lo = jnp.concatenate([block(lhs_lo, i) for i in order[span]], axis=0)
         y = lax.dot_general(hi, p_hi[...], contract, preferred_element_type=jnp.float32)
         y += lax.dot_general(hi, p_lo[...], contract, preferred_element_type=jnp.float32)
         y += lax.dot_general(lo, p_hi[...], contract, preferred_element_type=jnp.float32)
@@ -212,14 +219,13 @@
         c_swap(n).wait_recv()
         c_red[span] = part[span, core] + c_take[span]
         for k in range(many * n, many * n + many):
-            @pl.when(target(k) != chip)
-            def _():
+            if order[k]:
                 c_piece(k).start()
     most = c_got.at[pl.ds(0, CHIPS - 1)]
     pltpu.make_async_copy(most, most, c_sems.at[1]).wait()
-    total = c_red[lax.rem(col - chip + 7 + 2 * DEPTH, DEPTH)]
-    for i in range(CHIPS):
-        total += jnp.where(chip == i, jnp.zeros_like(total), c_got[i])
+    total = c_red[CHIPS - 1]
+    for k in range(CHIPS - 1):
+        total += c_got[k]
     for s in (0, 1):
         rows = pl.ds(s, 32, stride=2)
         out_ref[rows, :] = diag_ref[rows, :] + total[:, 64 * s : 64 * s + 64]
@@ -288,7 +294,7 @@
             pltpu.VMEM((DEPTH, 32, LANES), f32),
             pltpu.VMEM((DEPTH, 32, LANES), f32),
             pltpu.VMEM((CHIPS, 32, LANES), f32),
-            dma((4,)), dma((DEPTH + 1,)), dma((DEPTH + 1,)), dma((9,)), dma((9,)), dma((9,)), dma((9,)), dma, dma, dma((PARTS,)), dma((PARTS,)), dma((2,)),
+            dma((4,)), dma((DEPTH + 1,)), dma((DEPTH + 1,)), dma((9,)), dma((9,)), dma((9,)), dma((9,)), dma, dma, dma((PARTS,)), dma((PARTS,)), dma((2,)), pltpu.SemaphoreType.REGULAR,
         ],
         compiler_params=pltpu.CompilerParams(collective_id=0, has_side_effects=True, vmem_limit_bytes=63 * 2**20),
         cost_estimate=pl.CostEstimate(flops=3 * 2 * 84 * 2**20, bytes_accessed=2**20, transcendentals=0),

time: 60.1 us -> 57.7 us (0.960)
  Pallas kernels: 58.8 us -> 56.6 us
    pallas_call x1, Pallas kernels: 57.3 us -> 55.1 us  [local(): pl.pallas_call(kernel, out_shape=(jax.ShapeDtypeStruct((128, 128), f32),...]
where the time goes in v3:
time: 57.7 us; the launch traced here: 57.3 us
  Pallas kernels  56.6 us (98%)
  between operations  0.64 us (1%)
    pallas_call x1, Pallas kernels, local(): pl.pallas_call(kernel, out_shape=(jax.ShapeDtypeStruct((128, 128), f32),...  55.1 us
    pallas_call x1, Pallas kernels, local(): pl.pallas_call(hand_out, out_shape=(jax.ShapeDtypeStruct((128, 128), f32)...  1.49 us

profile of v3, /device:TPU:1, one launch (start us, length us, event | category | flops | bytes accessed | tf_op | source)
XLA Modules:
  0.0 57.3 jit_solution(5552202124448290763)
XLA Ops:
  0.6 55.1 %shard_map.59 = (f32[128,128]{1,0:T(8,128)}, f32[64,64]{1,0:T(8,128)}) custom-call(f32[128,256]{1,0:T(8,128)} %a_hbm.1, f32[128,128]{1,0:T(8,128)} %bitcast.6, s32[2,32]{1,0:T(2,128)} %mask_hbm.1, f32[64,64]{1,0:T(8,128)} %bitcast.8), custom_call_target="tpu_custom_call" | custom-call | flops 528482304 | bytes 1048576 | tf_op jit(solution)/shard_map/pallas_call | solution.py:269
  55.8 1.5 %shard_map.60 = (f32[128,128]{1,0:T(8,128)}, f32[64,64]{1,0:T(8,128)}) custom-call(f32[128,128]{1,0:T(8,128)} %get-tuple-element.6.panel_in, f32[64,64]{1,0:T(8,128)} %get-tuple-element.7.out_in), custom_call_target="tpu_custom_call" | custom-call | tf_op jit(solution)/shard_map/pallas_call | solution.py:303

commit v4 on v3

--- a/solution.py
+++ b/solution.py
@@ -172,7 +172,7 @@
     hand_on(0)
     for i in (4, 8, 12):
         pl.semaphore_signal(ready, inc=1, device_id=(in_plane(i) * 2 + core, col), device_id_type=MESH)
-    stages = [(0, multiply), (2, arrive), (2, multiply), (1, arrive), (0, scatter), (1, multiply), (2, scatter), (4, arrive), (4, multiply), (1, scatter), (3, arrive), (3, multiply), (4, scatter), (0, finish), (6, arrive), (6, multiply), (3, scatter), (2, finish), (5, arrive), (5, multiply), (6, scatter), (1, finish), (5, scatter), (4, finish), (8, arrive), (8, multiply), (7, arrive), (7, multiply), (8, scatter), (7, scatter), (3, finish), (6, finish), (5, finish), (8, finish), (7, finish)]
+    stages = [(0, multiply), (2, arrive), (2, multiply), (1, arrive), (1, multiply), (0, scatter), (2, scatter), (4, arrive), (4, multiply), (1, scatter), (3, arrive), (3, multiply), (4, scatter), (0, finish), (6, arrive), (6, multiply), (3, scatter), (2, finish), (5, arrive), (5, multiply), (6, scatter), (1, finish), (5, scatter), (4, finish), (8, arrive), (8, multiply), (7, arrive), (7, multiply), (8, scatter), (7, scatter), (3, finish), (6, finish), (5, finish), (8, finish), (7, finish)]
     for t, what in stages:
         what(t)
 

time: 57.7 us -> 57.1 us (0.990)
  no operation moved by 1% of the time
where the time goes in v4:
time: 57.1 us; the launch traced here: 56.9 us
  Pallas kernels  56.3 us (99%)
  between operations  0.64 us (1%)
    pallas_call x1, Pallas kernels, local(): pl.pallas_call(kernel, out_shape=(jax.ShapeDtypeStruct((128, 128), f32),...  54.8 us
    pallas_call x1, Pallas kernels, local(): pl.pallas_call(hand_out, out_shape=(jax.ShapeDtypeStruct((128, 128), f32)...  1.49 us

profile of v4, /device:TPU:1, one launch (start us, length us, event | category | flops | bytes accessed | tf_op | source)
XLA Modules:
  0.0 56.9 jit_solution(9176799440584844926)
XLA Ops:
  0.6 54.8 %shard_map.59 = (f32[128,128]{1,0:T(8,128)}, f32[64,64]{1,0:T(8,128)}) custom-call(f32[128,256]{1,0:T(8,128)} %a_hbm.1, f32[128,128]{1,0:T(8,128)} %bitcast.6, s32[2,32]{1,0:T(2,128)} %mask_hbm.1, f32[64,64]{1,0:T(8,128)} %bitcast.8), custom_call_target="tpu_custom_call" | custom-call | flops 528482304 | bytes 1048576 | tf_op jit(solution)/shard_map/pallas_call | solution.py:269
  55.4 1.5 %shard_map.60 = (f32[128,128]{1,0:T(8,128)}, f32[64,64]{1,0:T(8,128)}) custom-call(f32[128,128]{1,0:T(8,128)} %get-tuple-element.6.panel_in, f32[64,64]{1,0:T(8,128)} %get-tuple-element.7.out_in), custom_call_target="tpu_custom_call" | custom-call | tf_op jit(solution)/shard_map/pallas_call | solution.py:303
